TPU v7x, 32 devices: a whole 2x2x4 slice. The times are simulated.
32 devices in a mesh: seq: 8 (over z, x), tp: 4 (over y, core).
Axes of the slice: x: 2, y: 2, z: 4, core: 2. Of those that a mesh axis runs over, the one named last changes fastest.
Arguments:
- hidden: bfloat16 [2048, 8192], P('seq', 'tp'), may hold values from -6 to 6
- query_base: bfloat16 [2048, 4096], P('seq', 'tp'), may hold values from -150 to 150
- rotated_key_cache: bfloat16 [2048, 1024], P('seq', 'tp'), may hold values from -7 to 7
- frozen_value_base: bfloat16 [2048, 1024], P('seq', 'tp'), may hold values from -6 to 6
- output_cotangent: bfloat16 [2048, 4096], P('seq', 'tp'), may hold values from -0.9 to 0.9
- qdown_mean: float32 [16, 8192], P(None, 'tp'), may hold values from -0.0625 to 0.0625
- qdown_sigma: float32 [16, 8192], P(None, 'tp'), may hold values from 0.004 to 0.012
- qdown_noise: float32 [16, 8192], P(None, 'tp'), may hold values from -4 to 4
- qup_mean: float32 [16, 4096], P(None, 'tp'), may hold values from -1.5 to 1.5
- qup_sigma: float32 [16, 4096], P(None, 'tp'), may hold values from 0.08 to 0.25
- qup_noise: float32 [16, 4096], P(None, 'tp'), may hold values from -4 to 4
- vdown_mean: float32 [16, 8192], P(None, 'tp'), may hold values from -0.0625 to 0.0625
- vdown_sigma: float32 [16, 8192], P(None, 'tp'), may hold values from 0.004 to 0.012
- vdown_noise: float32 [16, 8192], P(None, 'tp'), may hold values from -4 to 4
- value_up_mean: float32 [16, 1024], P(None, 'tp'), may hold values from -1.5 to 1.5
- value_up_deviation: float32 [16, 1024], P(None, 'tp'), may hold values from 0.08 to 0.25
- value_up_noise: float32 [16, 1024], P(None, 'tp'), may hold values from -4 to 4
Outputs:
- qdown_gmean: float32 [16, 8192], P(None, 'tp')
- qdown_gsigma: float32 [16, 8192], P(None, 'tp')
- qup_gmean: float32 [16, 4096], P(None, 'tp')
- qup_gsigma: float32 [16, 4096], P(None, 'tp')
- vdown_gmean: float32 [16, 8192], P(None, 'tp')
- vdown_gsigma: float32 [16, 8192], P(None, 'tp')
- vup_gmean: float32 [16, 1024], P(None, 'tp')
- vup_gsigma: float32 [16, 1024], P(None, 'tp')
All inputs are finite; a program needn't handle non-finite values.
Results may differ from a plain program's by a relative error of at most 0.0075.
The roundings to bfloat16 on the way count: a program that leaves them out, or rounds other values in their place, can miss the bound.
Values may be sent and summed in bfloat16 or wider, within the bound.
A program may use at most 64 MiB of HBM per device.

v0:
```python
import jax
import jax.numpy as jnp
from jax import lax
from jax.sharding import PartitionSpec as P

QUERY_HEADS = 32
KEY_VALUE_HEADS = 8
HEAD_SIZE = 128


key_span = 512
row_groups = 4


def sample(mean, sigma, noise):
    return (mean + sigma * noise).astype(jnp.bfloat16)


def keep(state):
    return state


def blockwise(carry, key_piece, value_piece, update):
    count = key_piece.shape[0]
    steps = count // key_span
    key_blocks = key_piece.reshape(steps, key_span, key_piece.shape[1])
    value_blocks = value_piece.reshape(steps, key_span, value_piece.shape[1])

    def advance(state, inputs):
        key_blk, value_blk, index = inputs
        return (update(state, key_blk, value_blk, index * key_span), None)

    carry, unused = lax.scan(
        advance, carry, (key_blocks, value_blocks, jnp.arange(steps, dtype=jnp.int32))
    )
    return carry


def per_device(
    hidden,
    query_base,
    rotated_key_cache,
    frozen_value_base,
    output_cotangent,
    qdown_mean,
    qdown_sigma,
    qdown_noise,
    qup_mean,
    qup_sigma,
    qup_noise,
    vdown_mean,
    vdown_sigma,
    vdown_noise,
    value_up_mean,
    value_up_deviation,
    value_up_noise,
):
    scale = HEAD_SIZE ** (-0.5)
    query_group = QUERY_HEADS // KEY_VALUE_HEADS
    tokens = hidden.shape[0]
    kv_loc = rotated_key_cache.shape[1] // HEAD_SIZE
    nseq = lax.axis_size("seq")
    me_seq = lax.axis_index("seq")
    qdown = sample(qdown_mean, qdown_sigma, qdown_noise)
    qup = sample(qup_mean, qup_sigma, qup_noise)
    vdown = sample(vdown_mean, vdown_sigma, vdown_noise)
    vup = sample(value_up_mean, value_up_deviation, value_up_noise)
    low_parts = lax.psum(
        (
            jnp.dot(hidden, qdown.T, preferred_element_type=jnp.float32),
            jnp.dot(hidden, vdown.T, preferred_element_type=jnp.float32),
        ),
        "tp",
    )
    qlow = low_parts[0].astype(jnp.bfloat16)
    vlow = low_parts[1].astype(jnp.bfloat16)
    query_input = (
        query_base.astype(jnp.float32) + jnp.dot(qlow, qup, preferred_element_type=jnp.float32)
    ).astype(jnp.bfloat16)
    value_input = (
        frozen_value_base.astype(jnp.float32)
        + jnp.dot(vlow, vup, preferred_element_type=jnp.float32)
    ).astype(jnp.bfloat16)
    local = jnp.arange(tokens, dtype=jnp.int32)
    query_rows, grad_rows = (query_input, output_cotangent)
    positions = me_seq * tokens + local
    rows = tokens * query_group
    width = rows // row_groups
    head_queries = (
        query_rows.reshape(tokens, kv_loc, query_group, HEAD_SIZE)
        .transpose(1, 0, 2, 3)
        .reshape(kv_loc, rows, HEAD_SIZE)
    )
    head_output_gradient = (
        grad_rows.reshape(tokens, kv_loc, query_group, HEAD_SIZE)
        .transpose(1, 0, 2, 3)
        .reshape(kv_loc, rows, HEAD_SIZE)
    )
    row_pos = jnp.repeat(positions, query_group)
    limits = row_pos.reshape(row_groups, width).max(axis=1)

    def stats_update(carry, key_blk, value_blk, key_start):
        count = key_blk.shape[0]
        key_rows = key_blk.reshape(count, kv_loc, HEAD_SIZE)
        values = value_blk.reshape(count, kv_loc, HEAD_SIZE)
        key_pos = key_start + jnp.arange(count, dtype=jnp.int32)
        parts = []
        for index in range(row_groups):
            lower = index * width
            upper = lower + width
            state = tuple((item[:, lower:upper] for item in carry))

            def stats_refresh(state, lower=lower, upper=upper):
                top, total, weighted = state
                scores = (
                    jnp.einsum(
                        "krd,nkd->krn",
                        head_queries[:, lower:upper],
                        key_rows,
                        preferred_element_type=jnp.float32,
                    )
                    * scale
                )
                dprob = jnp.einsum(
                    "krd,nkd->krn",
                    head_output_gradient[:, lower:upper],
                    values,
                    preferred_element_type=jnp.float32,
                )
                mask = key_pos[None, None, :] <= row_pos[None, lower:upper, None]
                masked = jnp.where(mask, scores, -jnp.inf)
                fresh = jnp.maximum(top, jnp.max(masked, axis=2))
                weights = jnp.exp(masked - fresh[..., None])
                decay = jnp.exp(top - fresh)
                return (
                    fresh,
                    total * decay + jnp.sum(weights, axis=2),
                    weighted * decay + jnp.sum(weights * dprob, axis=2),
                )

            parts.append(lax.cond(key_start <= limits[index], stats_refresh, keep, state))
        return tuple((jnp.concatenate([part[item] for part in parts], axis=1) for item in range(3)))

    stats_init = (
        jnp.full((kv_loc, rows), -1e30, jnp.float32),
        jnp.zeros((kv_loc, rows), jnp.float32),
        jnp.zeros((kv_loc, rows), jnp.float32),
    )
    pieces = (
        lax.all_gather(rotated_key_cache, "seq", axis=0, tiled=True),
        lax.all_gather(value_input, "seq", axis=0, tiled=True),
    )
    top, total, weighted = blockwise(stats_init, pieces[0], pieces[1], stats_update)
    lse = top + jnp.log(total)
    delta = weighted / total

    def grads_block(dquery, key_blk, value_blk, key_start):
        count = key_blk.shape[0]
        key_rows = key_blk.reshape(count, kv_loc, HEAD_SIZE)
        values = value_blk.reshape(count, kv_loc, HEAD_SIZE)
        key_pos = key_start + jnp.arange(count, dtype=jnp.int32)
        value_sum = jnp.zeros((count, kv_loc, HEAD_SIZE), jnp.float32)
        parts = []
        for index in range(row_groups):
            lower = index * width
            upper = lower + width

            def grads_refresh(state, lower=lower, upper=upper):
                acc_query, acc_value = state
                scores = (
                    jnp.einsum(
                        "krd,nkd->krn",
                        head_queries[:, lower:upper],
                        key_rows,
                        preferred_element_type=jnp.float32,
                    )
                    * scale
                )
                dprob = jnp.einsum(
                    "krd,nkd->krn",
                    head_output_gradient[:, lower:upper],
                    values,
                    preferred_element_type=jnp.float32,
                )
                mask = key_pos[None, None, :] <= row_pos[None, lower:upper, None]
                masked = jnp.where(mask, scores, -jnp.inf)
                probs = jnp.exp(masked - lse[:, lower:upper, None])
                dscore = (probs * (dprob - delta[:, lower:upper, None])).astype(jnp.bfloat16)
                acc_query = (
                    acc_query
                    + jnp.einsum(
                        "krn,nkd->krd", dscore, key_rows, preferred_element_type=jnp.float32
                    )
                    * scale
                )
                acc_value = acc_value + jnp.einsum(
                    "krn,krd->nkd",
                    probs.astype(jnp.bfloat16),
                    head_output_gradient[:, lower:upper],
                    preferred_element_type=jnp.float32,
                )
                return (acc_query, acc_value)

            acc_query, value_sum = lax.cond(
                key_start <= limits[index], grads_refresh, keep, (dquery[:, lower:upper], value_sum)
            )
            parts.append(acc_query)
        return (jnp.concatenate(parts, axis=1), value_sum.reshape(count, kv_loc * HEAD_SIZE))

    def grads_update(carry, key_blk, value_blk, key_start):
        dquery, value_gradient = carry
        count = key_blk.shape[0]
        dquery, value_sum = grads_block(dquery, key_blk, value_blk, key_start)
        current = lax.dynamic_slice_in_dim(value_gradient, key_start, count, 0)
        value_gradient = lax.dynamic_update_slice_in_dim(
            value_gradient, current + value_sum, key_start, 0
        )
        return (dquery, value_gradient)

    query_zero = jnp.zeros((kv_loc, rows, HEAD_SIZE), jnp.float32)
    grads_init = (query_zero, jnp.zeros((tokens * nseq, kv_loc * HEAD_SIZE), jnp.float32))
    pieces = (
        lax.all_gather(rotated_key_cache, "seq", axis=0, tiled=True),
        lax.all_gather(value_input, "seq", axis=0, tiled=True),
    )
    dquery, dvalue_all = blockwise(grads_init, pieces[0], pieces[1], grads_update)
    value_gradient = lax.psum_scatter(dvalue_all, "seq", scatter_dimension=0, tiled=True).astype(
        jnp.bfloat16
    )
    dquery = (
        dquery.astype(jnp.bfloat16)
        .reshape(kv_loc, tokens, query_group, HEAD_SIZE)
        .transpose(1, 0, 2, 3)
        .reshape(tokens, kv_loc * query_group * HEAD_SIZE)
    )
    qup_grad = jnp.dot(qlow.T, dquery, preferred_element_type=jnp.float32)
    vup_grad = jnp.dot(vlow.T, value_gradient, preferred_element_type=jnp.float32)
    low_grads = lax.psum(
        (
            jnp.dot(dquery, qup.T, preferred_element_type=jnp.float32),
            jnp.dot(value_gradient, vup.T, preferred_element_type=jnp.float32),
        ),
        "tp",
    )
    qlow_grad = low_grads[0].astype(jnp.bfloat16)
    vlow_grad = low_grads[1].astype(jnp.bfloat16)
    qdown_grad = jnp.dot(qlow_grad.T, hidden, preferred_element_type=jnp.float32)
    vdown_grad = jnp.dot(vlow_grad.T, hidden, preferred_element_type=jnp.float32)
    totals = lax.psum((qdown_grad, qup_grad, vdown_grad, vup_grad), "seq")
    return (
        totals[0],
        totals[0] * qdown_noise,
        totals[1],
        totals[1] * qup_noise,
        totals[2],
        totals[2] * vdown_noise,
        totals[3],
        totals[3] * value_up_noise,
    )


def solution(mesh):
    return jax.shard_map(
        per_device,
        mesh=mesh,
        in_specs=(
            P("seq", "tp"),
            P("seq", "tp"),
            P("seq", "tp"),
            P("seq", "tp"),
            P("seq", "tp"),
            P(None, "tp"),
            P(None, "tp"),
            P(None, "tp"),
            P(None, "tp"),
            P(None, "tp"),
            P(None, "tp"),
            P(None, "tp"),
            P(None, "tp"),
            P(None, "tp"),
            P(None, "tp"),
            P(None, "tp"),
            P(None, "tp"),
        ),
        out_specs=(
            P(None, "tp"),
            P(None, "tp"),
            P(None, "tp"),
            P(None, "tp"),
            P(None, "tp"),
            P(None, "tp"),
            P(None, "tp"),
            P(None, "tp"),
        ),
        check_vma=False,
    )
```

profile of v0, /device:TPU:0, one launch (start us, length us, event | category | flops | bytes accessed | tf_op | source)
XLA Modules:
  0.0 442.6 jit_solution(11901917900571803582)
XLA Ops:
  11.2 13.1 %all-reduce.2 = (bf16[256,16]{0,1:T(8,128)(2,1)S(1)}, bf16[256,16]{0,1:T(8,128)(2,1)S(1)}) all-reduce(f32[256,16]{0,1:T(8,128)S(1)} %convolution_bitcast_fusion.5, f32[256,16]{0,1:T(8,128)S(1)} %convolution_bitcast_fusion.4), channel_id=1, replica_groups=mesh['seq'=8,'tp'=4] {'tp'}, use_global_device_ids=true, to_apply=%region_0.0 | all-reduce | flops 8192 | bytes 49152 | tf_op jit(solution)/shard_map/psum | solution.py:68
  27.0 26.1 %all-gather.3.cloned.1.call-done = bf16[2048,256]{1,0:T(8,128)(2,1)} async-done(((bf16[256,256]{1,0:T(8,128)(2,1)}), bf16[2048,256]{1,0:T(8,128)(2,1)}) %all-gather.3.cloned.1.call-update) | async-done | bytes 1048592 | tf_op jit(solution)/shard_map/all_gather | solution.py:223
  53.2 2.3 copy.139
  55.5 39.4 %all-gather.5.cloned.1.call-done = bf16[2048,256]{1,0:T(8,128)(2,1)} async-done(((bf16[256,256]{1,0:T(8,128)(2,1)}), bf16[2048,256]{1,0:T(8,128)(2,1)}) %all-gather.5.cloned.1.call-update) | async-done | bytes 1048592 | tf_op jit(solution)/shard_map/all_gather | solution.py:224
  94.8 2.3 copy.140
  97.1 28.7 %while.28 = (s32[]{:T(128)}, f32[2,1024]{1,0:T(2,128)S(1)}, f32[2,1024]{1,0:T(2,128)S(1)}, f32[2,1024]{1,0:T(2,128)S(1)}, s32[4]{0:T(128)S(1)}, /*index=5*/s32[4...) while((s32[]{:T(128)}, f32[2,1024]{1,0:T(2,128)S(1)}, ...), condition=%wide.region_24.25_spmd.clone, body=%wide.region_3.24_spmd.clone.sunk | while | flops 545808896 | bytes 18108156 | solution.py:33
  126.7 1.6 broadcast_in_dim.111
  128.3 68.0 %while.29 = (s32[]{:T(128)}, f32[2,1024,128]{2,1,0:T(8,128)S(1)}, f32[2048,256]{0,1:T(8,128)}, s32[4]{0:T(128)S(1)}, s32[4]{0:T(128)S(1)}, /*index=5*/bf16[4,512...) while((s32[]{:T(128)}, f32[2,1024,128]{2,1,0:T(8,128)S(1)}, ...), condition=%wide.region_34.35_spmd.clone, body=%wide.region_25.34_spmd.clone.sunk | while | flops 1083441664 | bytes 40456060 | solution.py:33
  135.0 6.2 %conditional.28 = (f32[2,256,128]{2,1,0:T(8,128)}, f32[512,2,128]{2,0,1:T(8,128)S(1)}) conditional(s32[]{:T(128)} %convert_element_type.189, f32[2,256,128]{2,1,0:T(8,128)} %get-tuple-element.1282, (s32[512]{0:T(512)S(1)}, s32[1024]{0:T(1024)S(1)}, bf16[2,1024,128]{2,1,0:T(8,128)(2,1)}, bf16[512,2,128]{0,2,1:T(8,128)(2,1)S(1)}, ...), branch_computations={%region_26.26_spmd, %region_27.27_spmd} | conditional | flops 270532608 | bytes 9847852 | solution.py:204
  137.5 2.1 fusion.31
  139.6 1.6 convolution_bitcast_fusion
  141.2 6.0 %conditional.29 = ((f32[2,256,128]{2,1,0:T(8,128)}, f32[512,2,128]{2,0,1:T(8,128)S(1)})) conditional(s32[]{:T(128)} %convert_element_type.188, (f32[2,256,128]{2,1,0:T(8,128)}, f32[512,2,128]{2,0,1:T(8,128)S(1)}) %tuple.246, (s32[512]{0:T(512)S(1)}, s32[1024]{0:T(1024)S(1)}, bf16[2,1024,128]{2,1,0:T(8,128)(2,1)}, ...), branch_computations={%region_28.28_spmd, %region_29.29_spmd} | conditional | flops 270663680 | bytes 8275024 | solution.py:204
  141.4 2.3 fusion.41
  143.7 1.7 fusion.46
  145.5 1.7 fusion.44
  147.2 5.9 %conditional.30 = ((f32[2,256,128]{2,1,0:T(8,128)S(1)}, f32[512,2,128]{2,0,1:T(8,128)S(1)})) conditional(s32[]{:T(128)} %convert_element_type.187, (f32[2,256,128]{2,1,0:T(8,128)S(1)}, f32[512,2,128]{2,0,1:T(8,128)S(1)}) %tuple.314, (s32[512]{0:T(512)S(1)}, s32[1024]{0:T(1024)S(1)}, bf16[2,1024,128]{2,1,0:T(8,128)(2,1)}, ...), branch_computations={%region_30.30_spmd, %region_31.31_spmd} | conditional | flops 270663680 | bytes 6177816 | solution.py:204
  147.4 2.3 fusion.56
  149.7 1.7 fusion.61
  151.5 1.6 fusion.59
  153.8 4.3 conditional.31
  159.3 1.9 add_dynamic-update-slice_fusion.2
  171.0 2.0 add_dynamic-update-slice_fusion.2
  182.7 1.9 add_dynamic-update-slice_fusion.2
  194.4 1.9 add_dynamic-update-slice_fusion.2
  197.9 144.5 %reduce-scatter.2.cloned.1.call-done = f32[256,256]{0,1:T(8,128)} async-done(((f32[2048,256]{0,1:T(8,128)}), f32[256,256]{0,1:T(8,128)}) %reduce-scatter.2.cloned.1.call-update) | async-done | bytes 262160 | tf_op jit(solution)/shard_map/reduce_scatter | solution.py:227
  343.6 10.3 %all-reduce.1 = (bf16[256,16]{0,1:T(8,128)(2,1)S(1)}, bf16[256,16]{0,1:T(8,128)(2,1)S(1)}) all-reduce(f32[256,16]{0,1:T(8,128)S(1)} %fusion.109, f32[256,16]{0,1:T(8,128)S(1)} %fusion.87), channel_id=1, replica_groups=mesh['seq'=8,'tp'=4] {'tp'}, use_global_device_ids=true, to_apply=%region_35.36 | all-reduce | flops 8192 | bytes 49152 | tf_op jit(solution)/shard_map/psum | solution.py:238
  355.9 35.1 %psum.63 = f32[16,256]{1,0:T(8,128)S(1)} all-reduce(f32[16,256]{1,0:T(8,128)S(1)} %fusion.85), channel_id=1, replica_groups=mesh['seq'=8,'tp'=4] {'seq'}, use_global_device_ids=true, to_apply=%region_41.42 | all-reduce | flops 4096 | bytes 32768 | tf_op jit(solution)/shard_map/psum | solution.py:249
  391.6 35.2 %all-reduce.5.cloned.1.call-done = (f32[16,2048]{1,0:T(8,128)}, f32[16,1024]{1,0:T(8,128)}, f32[16,2048]{1,0:T(8,128)}) async-done(((f32[16,2048]{1,0:T(8,128)}, f32[16,1024]{1,0:T(8,128)}, f32[16,2048]{1,0:T(8,128)}), (f32[16,2048]{1,0:T(8,128)}, f32[16,1024]{1,0:T(8,128)}, f32[16,2048]{1,0:T(8,128)})) %all-reduce.5.cloned.1.call-update) | async-done | bytes 327696 | tf_op jit(solution)/shard_map/psum | solution.py:249
  428.3 1.6 mul.128
  429.9 1.6 mul.130
  431.4 1.6 copy.227
  434.5 1.6 copy.229
  (264 shorter events, 68.3 us)
Async XLA Ops:
  7.2 1.2 copy-start
  7.2 17.1 %copy-start.16 = (f32[16,256]{1,0:T(8,128)S(1)}, f32[16,256]{1,0:T(8,128)}, u32[]{:S(2)}) copy-start(f32[16,256]{1,0:T(8,128)} %param.53) | copy-start | bytes 49156
  7.2 17.1 %copy-start.24 = (f32[16,256]{1,0:T(8,128)S(1)}, f32[16,256]{1,0:T(8,128)}, u32[]{:S(2)}) copy-start(f32[16,256]{1,0:T(8,128)} %param.52) | copy-start | bytes 49156
  7.2 17.1 %copy-start.23 = (f32[16,256]{1,0:T(8,128)S(1)}, f32[16,256]{1,0:T(8,128)}, u32[]{:S(2)}) copy-start(f32[16,256]{1,0:T(8,128)} %param.51) | copy-start | bytes 49156
  7.2 17.1 %copy-start.13 = (bf16[256,256]{1,0:T(8,128)(2,1)S(1)}, bf16[256,256]{1,0:T(8,128)(2,1)}, u32[]{:S(2)}) copy-start(bf16[256,256]{1,0:T(8,128)(2,1)} %param.40) | copy-start | bytes 393220
  7.2 18.1 %copy-start.12 = (f32[16,1024]{1,0:T(8,128)S(1)}, f32[16,1024]{1,0:T(8,128)}, u32[]{:S(2)}) copy-start(f32[16,1024]{1,0:T(8,128)} %param.47) | copy-start | bytes 196612
  7.2 18.1 %copy-start.15 = (f32[16,1024]{1,0:T(8,128)S(1)}, f32[16,1024]{1,0:T(8,128)}, u32[]{:S(2)}) copy-start(f32[16,1024]{1,0:T(8,128)} %param.46) | copy-start | bytes 196612
  7.2 18.1 %copy-start.14 = (f32[16,1024]{1,0:T(8,128)S(1)}, f32[16,1024]{1,0:T(8,128)}, u32[]{:S(2)}) copy-start(f32[16,1024]{1,0:T(8,128)} %param.45) | copy-start | bytes 196612
  7.3 18.1 %copy-start.10 = (bf16[256,1024]{1,0:T(8,128)(2,1)S(1)}, bf16[256,1024]{1,0:T(8,128)(2,1)}, u32[]{:S(2)}) copy-start(bf16[256,1024]{1,0:T(8,128)(2,1)} %param.38) | copy-start | bytes 1572868
  7.3 45.9 %all-gather.3.cloned.1.call-start = ((), (), s32[]{:S(2)}) async-start(), calls=%async_computation.1 | async-start | bytes 1179648 | tf_op jit(solution)/shard_map/all_gather | solution.py:223
  8.0 86.8 %all-gather.5.cloned.1.call-start = ((), (), s32[]{:S(2)}) async-start(), calls=%async_computation.2 | async-start | bytes 1179648 | tf_op jit(solution)/shard_map/all_gather | solution.py:224
  11.2 15.0 %copy-start.11 = (bf16[256,1024]{1,0:T(8,128)(2,1)S(1)}, bf16[256,1024]{1,0:T(8,128)(2,1)}, u32[]{:S(2)}) copy-start(bf16[256,1024]{1,0:T(8,128)(2,1)} %param.41) | copy-start | bytes 1572868
  24.3 2.3 copy-start.19
  24.3 2.3 copy-start.21
  25.3 317.2 %reduce-scatter.2.cloned.1.call-start = ((), (), s32[]{:S(2)}) async-start(), calls=%async_computation.3 | async-start | bytes 2359296 | tf_op jit(solution)/shard_map/reduce_scatter | solution.py:227
  125.8 0.8 copy-start.6
  136.5 1.0 copy-start.1
  141.2 6.0 %copy-start.2 = (f32[2,256,128]{2,1,0:T(8,128)S(1)}, f32[2,256,128]{2,1,0:T(8,128)}, u32[]{:S(2)}) copy-start(f32[2,256,128]{2,1,0:T(8,128)} %get-tuple-element.1278) | copy-start | bytes 786436 | tf_op jit(solution)/shard_map/while
  141.2 2.5 copy-start.4
  145.4 1.8 copy-start.5
  153.1 0.7 copy-start.3
  167.9 1.0 copy-start.2
  179.7 1.0 copy-start.2
  191.3 1.0 copy-start.2
  196.3 0.7 copy-start.20
  196.4 230.4 %all-reduce.5.cloned.1.call-start = ((), (), s32[]{:S(2)}) async-start(), calls=%async_computation.4 | async-start | bytes 655360 | tf_op jit(solution)/shard_map/psum | solution.py:249
  196.8 159.0 %copy-start.22 = (bf16[256,16]{0,1:T(8,128)(2,1)S(1)}, bf16[256,16]{0,1:T(8,128)(2,1)}, u32[]{:S(2)}) copy-start(bf16[256,16]{0,1:T(8,128)(2,1)} %copy-done.21) | copy-start | bytes 24580
  197.0 193.9 %copy-start.17 = (f32[16,256]{1,0:T(8,128)S(1)}, f32[16,256]{1,0:T(8,128)}, u32[]{:S(2)}) copy-start(f32[16,256]{1,0:T(8,128)} %param.53) | copy-start | bytes 49156
  197.1 231.2 %copy-start.8 = (f32[16,2048]{1,0:T(8,128)S(1)}, f32[16,2048]{1,0:T(8,128)}, u32[]{:S(2)}) copy-start(f32[16,2048]{1,0:T(8,128)} %param.44) | copy-start | bytes 393220
  197.9 231.9 %copy-start.9 = (f32[16,2048]{1,0:T(8,128)S(1)}, f32[16,2048]{1,0:T(8,128)}, u32[]{:S(2)}) copy-start(f32[16,2048]{1,0:T(8,128)} %param.50) | copy-start | bytes 393220
  342.4 13.3 %copy-start.7 = (f32[256,256]{0,1:T(8,128)S(1)}, f32[256,256]{0,1:T(8,128)}, u32[]{:S(2)}) copy-start(f32[256,256]{0,1:T(8,128)} %reduce-scatter.2.cloned.1.call-done) | copy-start | bytes 786436
  391.0 45.1 %copy-start.18 = (f32[16,256]{1,0:T(8,128)}, f32[16,256]{1,0:T(8,128)S(1)}, u32[]{:S(2)}) copy-start(f32[16,256]{1,0:T(8,128)S(1)} %psum.63) | copy-start | bytes 49156
  (3 other events, 2.1 us)
Sparse Core Ops, SparseCore 0:
  10.2 42.9 all-gather.2
  55.9 38.8 all-gather.4
  196.5 145.9 reduce-scatter.1
  355.8 70.8 all-reduce.4
where the time goes:
time: 445 us; the launch traced here: 443 us
  waiting for transfers between devices  246 us (55%)
  blocking collectives  58.4 us (13%)
  local copies, waits for them, and re-layouts  45.2 us (10%)
  matrix products  30.9 us (7%)
  loops' own time  27.2 us (6%)
  other arithmetic  20.6 us (5%)
  between operations  14.1 us (3%)
    reduce_scatter x1, waiting for transfers between devices, per_device(): lax.psum_scatter(dvalue_all, 'seq', scatter_dimension=0, tiled=True)  144 us
    all_gather x1, waiting for transfers between devices, per_device(): lax.all_gather(value_input, 'seq', axis=0, tiled=True)  39.4 us
    psum x1, waiting for transfers between devices, per_device(): totals = lax.psum((qdown_grad, qup_grad, vdown_grad, vup_grad), 'seq')  35.2 us
    psum x1, blocking collectives, per_device(): totals = lax.psum((qdown_grad, qup_grad, vdown_grad, vup_grad), 'seq')  35.1 us
    another operation x2, loops' own time, blockwise(): lax.scan(advance, carry, (key_blocks, value_blocks, jnp.arange(steps, dty...  26.7 us
    all_gather x1, waiting for transfers between devices, per_device(): lax.all_gather(rotated_key_cache, 'seq', axis=0, tiled=True)  26.1 us
    dynamic_slice x16, local copies, waits for them, and re-layouts, blockwise(): lax.scan(advance, carry, (key_blocks, value_blocks, jnp.arange(steps, dty...  13.2 us
    psum x1, blocking collectives, per_device(): lax.psum((jnp.dot(hidden, qdown.T, preferred_element_type=jnp.float32), j...  13.1 us
  transfers between devices with their start and end apart: 4, of which 4 were waited for; matrix products, arithmetic and copies ran while one was open for 2% of the time, Pallas kernels for 0%

commit v1 on v0

v1 whole, which is shorter than its diff:
```python
import functools
import math

import jax
import jax.numpy as jnp
from jax import lax
from jax.experimental import pallas as pl
from jax.experimental.pallas import tpu as pltpu
from jax.sharding import PartitionSpec as P

HEAD = 128
RANK = 16
GROUP = 4
F32 = jnp.float32
BF16 = jnp.bfloat16
NEG = -1e30


def nt(a, b):
    return lax.dot_general(a, b, (((1,), (1,)), ((), ())), preferred_element_type=F32)


def tn(a, b):
    return lax.dot_general(a, b, (((0,), (0,)), ((), ())), preferred_element_type=F32)


def nn(a, b):
    return jnp.dot(a, b, preferred_element_type=F32)


def kernel(
    n, m, units, per,
    hidden, qbase, kc, vb, og,
    qdm, qds, qdn, qum, qus, qun, vdm, vds, vdn, vum, vus, vun,
    o_qd, o_qds, o_qu, o_qus, o_vd, o_vds, o_vu, o_vus,
    kall, vall, vlow_all, lowx, gx, qs, dos, top, tot, wei, dqt, vgs, vgx, vug, quw, pack, rsx, agx,
    k_s, k_r, v_s, v_r, l_s, l_r, x_s, x_r, y_s, y_r, g_s, g_r, r_s, r_r, a_s, a_r,
):
    T, DL = hidden.shape
    KV = kc.shape[1] // HEAD
    rows = GROUP * T
    scale = HEAD ** -0.5
    c2 = scale * math.log2(math.e)
    me = lax.axis_index("seq")
    t = lax.axis_index("tp")

    def to_seq(src, dst, ss, rs, who):
        return pltpu.make_async_remote_copy(
            src_ref=src, dst_ref=dst, send_sem=ss, recv_sem=rs,
            device_id=(who, t), device_id_type=pl.DeviceIdType.MESH,
        )

    def to_tp(src, dst, ss, rs, who):
        return pltpu.make_async_remote_copy(
            src_ref=src, dst_ref=dst, send_sem=ss, recv_sem=rs,
            device_id=(me, who), device_id_type=pl.DeviceIdType.MESH,
        )

    def loop(lo, hi, body):
        def step(i, c):
            body(i)
            return c
        lax.fori_loop(lo, hi, step, 0)

    barrier = pltpu.get_barrier_semaphore()

    def greet_seq(d):
        pl.semaphore_signal(
            barrier, inc=1, device_id=(lax.rem(me + d, n), t),
            device_id_type=pl.DeviceIdType.MESH,
        )

    def greet_tp(d):
        pl.semaphore_signal(
            barrier, inc=1, device_id=(me, lax.rem(t + d, m)),
            device_id_type=pl.DeviceIdType.MESH,
        )

    loop(1, n, greet_seq)
    loop(1, m, greet_tp)
    pl.semaphore_wait(barrier, n + m - 2)

    def k_copy(who):
        return to_seq(kc, kall.at[me], k_s.at[who], k_r.at[me], who)

    def v_copy(who):
        return to_seq(vb, vall.at[me], v_s.at[who], v_r.at[me], who)

    def send_kv(who):
        k_copy(who).start()
        v_copy(who).start()

    loop(me + 1, n, send_kv)

    qup = (qum[...] + qus[...] * qun[...]).astype(BF16)
    vup = (vum[...] + vus[...] * vun[...]).astype(BF16)
    qdown = (qdm[...] + qds[...] * qdn[...]).astype(BF16)
    vdown = (vdm[...] + vds[...] * vdn[...]).astype(BF16)
    lowx[t] = jnp.concatenate([nt(qdown, hidden[...]), nt(vdown, hidden[...])], axis=0)

    def x_copy(who):
        return to_tp(lowx.at[t], lowx.at[t], x_s.at[who], x_r.at[t], who)

    def x_in(who):
        return to_tp(lowx.at[who], lowx.at[who], x_s.at[who], x_r.at[who], who)

    loop(1, m, lambda d: x_copy(lax.rem(t + d, m)).start())
    for g in range(KV):
        for h in range(GROUP):
            at = (g * GROUP + h) * HEAD
            dos[g, h * T:(h + 1) * T, :] = og[:, at:at + HEAD]
    loop(1, m, lambda d: x_in(lax.rem(t + d, m)).wait_recv())
    low = lowx[0]
    for i in range(1, m):
        low = low + lowx[i]
    low = low.astype(BF16)
    qlow = low[:RANK]
    vlow = low[RANK:]
    vlow_all[me] = vlow

    def l_copy(who):
        return to_seq(vlow_all.at[me], vlow_all.at[me], l_s.at[who], l_r.at[me], who)

    loop(me + 1, n, lambda who: l_copy(who).start())

    for g in range(KV):
        for h in range(GROUP):
            at = (g * GROUP + h) * HEAD
            q = qbase[:, at:at + HEAD].astype(F32) + tn(qlow, qup[:, at:at + HEAD])
            qs[g, h * T:(h + 1) * T, :] = q.astype(BF16)

    kall[me] = kc[...]
    vall[me] = vb[...]
    key_pos = lax.broadcasted_iota(jnp.int32, (T, rows), 0)
    row_pos = lax.broadcasted_iota(jnp.int32, (T, rows), 1) % T
    seen = key_pos <= row_pos

    def make_value(j):
        vall[j] = (vall[j].astype(F32) + tn(vlow_all[j], vup)).astype(BF16)

    def stats(j, first):
        for g in range(KV):
            cols = slice(g * HEAD, (g + 1) * HEAD)
            s = nt(kall[j, :, cols], qs[g]) * c2
            dp = nt(vall[j, :, cols], dos[g])
            if first:
                s = jnp.where(seen, s, NEG)
                new = jnp.max(s, axis=0, keepdims=True)
                e = jnp.exp2(s - new)
                tot[g] = jnp.sum(e, axis=0, keepdims=True)
                wei[g] = jnp.sum(e * dp, axis=0, keepdims=True)
            else:
                old = top[g]
                new = jnp.maximum(old, jnp.max(s, axis=0, keepdims=True))
                e = jnp.exp2(s - new)
                decay = jnp.exp2(old - new)
                tot[g] = tot[g] * decay + jnp.sum(e, axis=0, keepdims=True)
                wei[g] = wei[g] * decay + jnp.sum(e * dp, axis=0, keepdims=True)
            top[g] = new

    make_value(me)
    stats(me, True)

    def stats_step(i):
        j = me - i
        to_seq(kc, kall.at[j], k_s.at[j], k_r.at[j], j).wait_recv()
        to_seq(vb, vall.at[j], v_s.at[j], v_r.at[j], j).wait_recv()
        to_seq(vlow_all.at[j], vlow_all.at[j], l_s.at[j], l_r.at[j], j).wait_recv()
        make_value(j)
        stats(j, False)

    loop(1, me + 1, stats_step)

    for g in range(KV):
        total = tot[g]
        top[g] = top[g] + jnp.log2(total)
        wei[g] = wei[g] / total

    def grads(j, first):
        part = jnp.zeros((RANK, T), F32)
        for g in range(KV):
            cols = slice(g * HEAD, (g + 1) * HEAD)
            key = kall[j, :, cols]
            s = nt(key, qs[g]) * c2
            dp = nt(vall[j, :, cols], dos[g])
            if first:
                s = jnp.where(seen, s, NEG)
            p = jnp.exp2(s - top[g])
            ds = (p * (dp - wei[g])).astype(BF16)
            dq = tn(key, ds)
            dv = nn(p.astype(BF16), dos[g]).astype(BF16)
            part = part + nt(vup[:, cols], dv)
            vu = nn(vlow_all[j], dv)
            if first:
                dqt[g] = dq
                vug[g] = vu
            else:
                dqt[g] += dq
                vug[g] += vu
        vgs[j] = part

    grads(me, True)

    def g_copy(j):
        return to_seq(vgs.at[j], vgx.at[me], g_s.at[j], g_r.at[me], j)

    def grads_step(i):
        j = me - i
        grads(j, False)
        g_copy(j).start()

    loop(1, me + 1, grads_step)

    qg = jnp.zeros((RANK, T), F32)
    for g in range(KV):
        for h in range(GROUP):
            at = (g * GROUP + h) * HEAD
            dq = (dqt[g, :, h * T:(h + 1) * T] * scale).astype(BF16)
            qg = qg + nn(qup[:, at:at + HEAD], dq)
            quw[:, at:at + HEAD] = nt(qlow, dq)

    def g_in(src):
        to_seq(vgs.at[src], vgx.at[src], g_s.at[src], g_r.at[src], src).wait_recv()

    loop(me + 1, n, g_in)
    vg = lax.fori_loop(me + 1, n, lambda s, acc: acc + vgx[s], vgs[me])
    gx[t] = jnp.concatenate([qg, vg], axis=0)

    def y_copy(who):
        return to_tp(gx.at[t], gx.at[t], y_s.at[who], y_r.at[t], who)

    def y_in(who):
        return to_tp(gx.at[who], gx.at[who], y_s.at[who], y_r.at[who], who)

    loop(1, m, lambda d: y_copy(lax.rem(t + d, m)).start())
    loop(1, m, lambda d: y_in(lax.rem(t + d, m)).wait_recv())
    lg = gx[0]
    for i in range(1, m):
        lg = lg + gx[i]
    dg = nn(lg.astype(BF16), hidden[...])

    outs = []
    for k in range(DL // HEAD):
        outs.append((dg[:RANK, k * HEAD:(k + 1) * HEAD], o_qd, o_qds, qdn, k))
    for k in range(DL // HEAD):
        outs.append((dg[RANK:, k * HEAD:(k + 1) * HEAD], o_vd, o_vds, vdn, k))
    for k in range(KV * GROUP):
        outs.append((quw[:, k * HEAD:(k + 1) * HEAD], o_qu, o_qus, qun, k))
    for k in range(KV):
        outs.append((vug[k], o_vu, o_vus, vun, k))
    for i in range(n * per):
        if i < units:
            pack[i // per, i % per] = outs[i][0].astype(BF16)
        else:
            pack[i // per, i % per] = jnp.zeros((RANK, HEAD), BF16)

    def r_copy(who):
        return to_seq(pack.at[who], rsx.at[me], r_s.at[who], r_r.at[me], who)

    def r_in(src):
        return to_seq(pack.at[src], rsx.at[src], r_s.at[src], r_r.at[src], src)

    loop(1, n, lambda d: r_copy(lax.rem(me + d, n)).start())
    rsx[me] = pack[me]
    loop(1, n, lambda d: r_in(lax.rem(me + d, n)).wait_recv())
    total = rsx[0].astype(F32)
    for i in range(1, n):
        total = total + rsx[i].astype(F32)
    agx[me] = total.astype(BF16)

    def a_copy(who):
        return to_seq(agx.at[me], agx.at[me], a_s.at[who], a_r.at[me], who)

    def a_in(src):
        return to_seq(agx.at[src], agx.at[src], a_s.at[src], a_r.at[src], src)

    loop(1, n, lambda d: a_copy(lax.rem(me + d, n)).start())
    loop(1, n, lambda d: a_in(lax.rem(me + d, n)).wait_recv())
    for i in range(units):
        _, mean, sigma, noise, k = outs[i]
        cols = slice(k * HEAD, (k + 1) * HEAD)
        value = agx[i // per, i % per].astype(F32)
        mean[:, cols] = value
        sigma[:, cols] = value * noise[:, cols]

    def drain_later(who):
        k_copy(who).wait_send()
        v_copy(who).wait_send()
        l_copy(who).wait_send()

    loop(me + 1, n, drain_later)
    loop(0, me, lambda j: g_copy(j).wait_send())

    def drain_tp(d):
        who = lax.rem(t + d, m)
        x_copy(who).wait_send()
        y_copy(who).wait_send()

    loop(1, m, drain_tp)

    def drain_seq(d):
        who = lax.rem(me + d, n)
        r_copy(who).wait_send()
        a_copy(who).wait_send()

    loop(1, n, drain_seq)


def solution(mesh):
    n = mesh.shape["seq"]
    m = mesh.shape["tp"]

    def step(*args):
        hidden, qbase, kc = args[:3]
        T, DL = hidden.shape
        QL, KL = qbase.shape[1], kc.shape[1]
        KV = KL // HEAD
        rows = GROUP * T
        units = (2 * DL + QL + KL) // HEAD
        per = -(-units // n)
        shape = lambda cols: jax.ShapeDtypeStruct((RANK, cols), F32)
        vmem = pl.BlockSpec(memory_space=pltpu.VMEM)
        sem = pltpu.SemaphoreType.DMA
        return tuple(pl.pallas_call(
            functools.partial(kernel, n, m, units, per),
            out_shape=[shape(c) for c in (DL, DL, QL, QL, DL, DL, KL, KL)],
            in_specs=[vmem] * 17,
            out_specs=[vmem] * 8,
            scratch_shapes=[
                pltpu.VMEM((n, T, KL), BF16),
                pltpu.VMEM((n, T, KL), BF16),
                pltpu.VMEM((n, RANK, T), BF16),
                pltpu.VMEM((m, 2 * RANK, T), F32),
                pltpu.VMEM((m, 2 * RANK, T), F32),
                pltpu.VMEM((KV, rows, HEAD), BF16),
                pltpu.VMEM((KV, rows, HEAD), BF16),
                pltpu.VMEM((KV, 1, rows), F32),
                pltpu.VMEM((KV, 1, rows), F32),
                pltpu.VMEM((KV, 1, rows), F32),
                pltpu.VMEM((KV, HEAD, rows), F32),
                pltpu.VMEM((n, RANK, T), F32),
                pltpu.VMEM((n, RANK, T), F32),
                pltpu.VMEM((KV, RANK, HEAD), F32),
                pltpu.VMEM((RANK, QL), F32),
                pltpu.VMEM((n, per, RANK, HEAD), BF16),
                pltpu.VMEM((n, per, RANK, HEAD), BF16),
                pltpu.VMEM((n, per, RANK, HEAD), BF16),
            ] + [sem((k,)) for k in (n, n, n, n, n, n, m, m, m, m, n, n, n, n, n, n)],
            compiler_params=pltpu.CompilerParams(
                collective_id=0, has_side_effects=True, vmem_limit_bytes=48 * 1024 * 1024
            ),
            cost_estimate=pl.CostEstimate(
                flops=14 * rows * KV * n * T * HEAD // 2,
                bytes_accessed=8 * 1024 * 1024,
                transcendentals=rows * KV * n * T,
            ),
        )(*args))

    wide = P("seq", "tp")
    flat = P(None, "tp")
    return jax.shard_map(
        step,
        mesh=mesh,
        in_specs=(wide,) * 5 + (flat,) * 12,
        out_specs=(flat,) * 8,
        check_vma=False,
    )
```

time: 445 us -> 113 us (0.25)
  waiting for transfers between devices: 246 us -> 0 us
  Pallas kernels: 0 us -> 91.3 us
  blocking collectives: 58.4 us -> 0 us
  matrix products: 30.9 us -> 0 us
  loops' own time: 27.2 us -> 0 us
  local copies, waits for them, and re-layouts: 45.2 us -> 20.3 us
  other arithmetic: 20.6 us -> 0 us
  between operations: 14.1 us -> 0.68 us
    reduce_scatter x1 -> x0, waiting for transfers between devices: 144 us -> none  [per_device(): lax.psum_scatter(dvalue_all, 'seq', scatter_dimension=0, tiled=True)]
    pallas_call x0 -> x1, Pallas kernels: none -> 91.3 us  [step(): pl.pallas_call(functools.partial(kernel, n, m, units, per), out_shape=[sh...]
    all_gather x2 -> x0, waiting for transfers between devices: 65.5 us -> none  [the longest x1 39.4 us: per_device(): lax.all_gather(value_input, 'seq', axis=0, tiled=True)]
    psum x3 -> x0, blocking collectives: 58.4 us -> none  [the longest x1 35.1 us: per_device(): totals = lax.psum((qdown_grad, qup_grad, vdown_grad, vup_grad), 'seq')]
    psum x1 -> x0, waiting for transfers between devices: 35.2 us -> none  [per_device(): totals = lax.psum((qdown_grad, qup_grad, vdown_grad, vup_grad), 'seq')]
    dot_general x30 -> x0, matrix products: 30.9 us -> none  [the longest x4 7.28 us: grads_refresh(): jnp.einsum('krd,nkd->krn', head_queries[:, lower:upper], key_rows, prefer...]
    another operation x34 -> x0, loops' own time: 27.2 us -> none  [the longest x2 26.7 us: blockwise(): lax.scan(advance, carry, (key_blocks, value_blocks, jnp.arange(steps, dty...]
    dynamic_slice x16 -> x0, local copies, waits for them, and re-layouts: 13.2 us -> none  [blockwise(): lax.scan(advance, carry, (key_blocks, value_blocks, jnp.arange(steps, dty...]
  transfers between devices with their start and end apart: 4 -> 0, of which waited for: 4 -> 0; matrix products, arithmetic and copies ran while one was open for 2% -> 0% of each run, Pallas kernels for 0% -> 0%
where the time goes in v1:
time: 113 us; the launch traced here: 112 us
  Pallas kernels  91.3 us (81%)
  local copies, waits for them, and re-layouts  20.3 us (18%)
    pallas_call x1, Pallas kernels, step(): pl.pallas_call(functools.partial(kernel, n, m, units, per), out_shape=[sh...  91.3 us
    unnamed x42, local copies, waits for them, and re-layouts  20.3 us

profile of v1, /device:TPU:0, one launch (start us, length us, event | category | flops | bytes accessed | tf_op | source)
XLA Modules:
  0.0 112.3 jit_solution(11972154536253446268)
XLA Ops:
  0.6 0.0 copy-start
  0.7 1.2 %copy-done = bf16[256,2048]{1,0:T(8,128)(2,1)S(1)} copy-done((bf16[256,2048]{1,0:T(8,128)(2,1)S(1)}, bf16[256,2048]{1,0:T(8,128)(2,1)}, u32[]{:S(2)}) %copy-start) | copy-done | bytes 1048600
  1.9 0.0 copy-start.1
  1.9 1.0 copy-done.1
  2.9 0.0 copy-start.2
  2.9 1.0 copy-done.2
  4.0 0.0 copy-start.3
  4.0 0.9 copy-done.3
  4.9 0.0 copy-start.4
  4.9 0.9 copy-done.4
  5.8 0.0 copy-start.5
  5.8 0.9 copy-done.5
  6.7 0.9 copy-done.6
  7.6 0.9 copy-done.7
  8.5 0.9 copy-done.8
  9.4 0.9 copy-done.9
  10.3 0.9 copy-done.10
  11.2 0.8 copy-done.11
  12.0 0.8 copy-done.12
  12.9 0.8 copy-done.13
  13.7 0.7 copy-done.14
  14.4 0.7 copy-done.15
  15.1 0.7 copy-done.16
  15.9 91.3 %shard_map.224 = (f32[16,2048]{1,0:T(8,128)S(1)}, f32[16,2048]{1,0:T(8,128)S(1)}, f32[16,1024]{1,0:T(8,128)S(1)}, f32[16,1024]{1,0:T(8,128)S(1)}, f32[16,2048]{1...) custom-call(bf16[256,2048]{1,0:T(8,128)(2,1)S(1)} %copy-done, ...), custom_call_target="tpu_custom_call" | custom-call | flops 3758096384 | bytes 8388608 | tf_op jit(solution)/shard_map/pallas_call | solution.py:324
  107.2 0.7 copy.33
  107.9 0.7 copy.34
  108.5 0.6 copy.35
  109.2 0.6 copy.36
  109.8 0.7 copy.37
  110.4 0.7 copy.38
  111.1 0.6 copy.39
  111.7 0.6 copy.40
  (11 shorter events, 0.0 us)
Async XLA Ops:
  0.6 1.2 %copy-start = (bf16[256,2048]{1,0:T(8,128)(2,1)S(1)}, bf16[256,2048]{1,0:T(8,128)(2,1)}, u32[]{:S(2)}) copy-start(bf16[256,2048]{1,0:T(8,128)(2,1)} %hidden.1) | copy-start | bytes 3145732
  1.9 1.0 copy-start.1
  2.9 1.0 copy-start.2
  4.0 0.9 copy-start.3
  4.9 0.9 copy-start.4
  5.8 0.9 copy-start.5
  6.7 0.9 copy-start.6
  7.6 0.9 copy-start.7
  8.5 0.9 copy-start.8
  9.4 0.9 copy-start.9
  10.3 0.9 copy-start.10
  11.2 0.8 copy-start.11
  12.0 0.8 copy-start.12
  12.9 0.8 copy-start.13
  13.7 0.7 copy-start.14
  14.4 0.7 copy-start.15
  15.1 0.7 copy-start.16

commit v2 on v1

--- a/solution.py
+++ b/solution.py
@@ -29,13 +29,20 @@
 
 
 def kernel(
-    n, m, units, per,
-    hidden, qbase, kc, vb, og,
-    qdm, qds, qdn, qum, qus, qun, vdm, vds, vdn, vum, vus, vun,
-    o_qd, o_qds, o_qu, o_qus, o_vd, o_vds, o_vu, o_vus,
-    kall, vall, vlow_all, lowx, gx, qs, dos, top, tot, wei, dqt, vgs, vgx, vug, quw, pack, rsx, agx,
+    n, m, units, per, X, *refs,
+):
+    sources = refs[:17]
+    held = refs[25:42]
+    loaded = refs[-1]
+    hidden, qbase, kc, vb, og, qdm, qds, qdn, qum, qus, qun, vdm, vds, vdn, vum, vus, vun = held
+    kc, vb = sources[2:4]
+    (
+        o_qd, o_qds, o_qu, o_qus, o_vd, o_vds, o_vu, o_vus,
+    ) = refs[17:25]
+    (
+    kall, vall, vval, vlow_all, lowx, gx, qs, dos, top, tot, wei, dqt, vgs, vgx, vug, quw, pack, rsx, agx,
     k_s, k_r, v_s, v_r, l_s, l_r, x_s, x_r, y_s, y_r, g_s, g_r, r_s, r_r, a_s, a_r,
-):
+    ) = refs[42:-1]
     T, DL = hidden.shape
     KV = kc.shape[1] // HEAD
     rows = GROUP * T
@@ -62,6 +69,18 @@
             return c
         lax.fori_loop(lo, hi, step, 0)
 
+    def load(i):
+        dst = held[i]
+        if i == 2:
+            dst = kall.at[me]
+        if i == 3:
+            dst = vall.at[me]
+        return pltpu.make_async_copy(sources[i], dst, loaded.at[i])
+
+    order = (0, 5, 6, 7, 11, 12, 13, 4, 1, 8, 9, 10, 14, 15, 16, 2, 3)
+    for i in order:
+        load(i).start()
+
     barrier = pltpu.get_barrier_semaphore()
 
     def greet_seq(d):
@@ -80,20 +99,33 @@
     loop(1, m, greet_tp)
     pl.semaphore_wait(barrier, n + m - 2)
 
-    def k_copy(who):
-        return to_seq(kc, kall.at[me], k_s.at[who], k_r.at[me], who)
-
-    def v_copy(who):
-        return to_seq(vb, vall.at[me], v_s.at[who], v_r.at[me], who)
-
-    def send_kv(who):
-        k_copy(who).start()
-        v_copy(who).start()
-
-    loop(me + 1, n, send_kv)
-
-    qup = (qum[...] + qus[...] * qun[...]).astype(BF16)
-    vup = (vum[...] + vus[...] * vun[...]).astype(BF16)
+    x = lax.rem(me, X)
+    plane = me - x
+
+    def kv(part, j, who, slot, own=False):
+        if part == 0:
+            return to_seq(kc if own else kall.at[j], kall.at[j], k_s.at[j, slot], k_r.at[j], who)
+        return to_seq(vb if own else vall.at[j], vall.at[j], v_s.at[j, slot], v_r.at[j], who)
+
+    def hand_on(j, part, own, act):
+        @pl.when(me + X < n)
+        def _():
+            act(kv(part, j, me + X, 0, own))
+
+        def across(d):
+            other = lax.rem(x + d, X)
+
+            @pl.when(plane + other > j)
+            def _():
+                act(kv(part, j, plane + other, 1 + other, own))
+
+        loop(1, X, across)
+
+    for part in range(2):
+        hand_on(me, part, True, lambda c: c.start())
+
+    for i in order[:7]:
+        load(i).wait()
     qdown = (qdm[...] + qds[...] * qdn[...]).astype(BF16)
     vdown = (vdm[...] + vds[...] * vdn[...]).astype(BF16)
     lowx[t] = jnp.concatenate([nt(qdown, hidden[...]), nt(vdown, hidden[...])], axis=0)
@@ -105,6 +137,10 @@
         return to_tp(lowx.at[who], lowx.at[who], x_s.at[who], x_r.at[who], who)
 
     loop(1, m, lambda d: x_copy(lax.rem(t + d, m)).start())
+    for i in order[7:]:
+        load(i).wait()
+    qup = (qum[...] + qus[...] * qun[...]).astype(BF16)
+    vup = (vum[...] + vus[...] * vun[...]).astype(BF16)
     for g in range(KV):
         for h in range(GROUP):
             at = (g * GROUP + h) * HEAD
@@ -129,20 +165,18 @@
             q = qbase[:, at:at + HEAD].astype(F32) + tn(qlow, qup[:, at:at + HEAD])
             qs[g, h * T:(h + 1) * T, :] = q.astype(BF16)
 
-    kall[me] = kc[...]
-    vall[me] = vb[...]
     key_pos = lax.broadcasted_iota(jnp.int32, (T, rows), 0)
     row_pos = lax.broadcasted_iota(jnp.int32, (T, rows), 1) % T
     seen = key_pos <= row_pos
 
     def make_value(j):
-        vall[j] = (vall[j].astype(F32) + tn(vlow_all[j], vup)).astype(BF16)
+        vval[j] = (vall[j].astype(F32) + tn(vlow_all[j], vup)).astype(BF16)
 
     def stats(j, first):
         for g in range(KV):
             cols = slice(g * HEAD, (g + 1) * HEAD)
             s = nt(kall[j, :, cols], qs[g]) * c2
-            dp = nt(vall[j, :, cols], dos[g])
+            dp = nt(vval[j, :, cols], dos[g])
             if first:
                 s = jnp.where(seen, s, NEG)
                 new = jnp.max(s, axis=0, keepdims=True)
@@ -161,15 +195,28 @@
     make_value(me)
     stats(me, True)
 
-    def stats_step(i):
-        j = me - i
-        to_seq(kc, kall.at[j], k_s.at[j], k_r.at[j], j).wait_recv()
-        to_seq(vb, vall.at[j], v_s.at[j], v_r.at[j], j).wait_recv()
+    def arrive(j):
         to_seq(vlow_all.at[j], vlow_all.at[j], l_s.at[j], l_r.at[j], j).wait_recv()
         make_value(j)
         stats(j, False)
 
-    loop(1, me + 1, stats_step)
+    def from_column(i):
+        j = me - i * X
+        for part in range(2):
+            kv(part, j, me, 0).wait_recv()
+            hand_on(j, part, False, lambda c: c.start())
+        arrive(j)
+
+    def from_across(j):
+        @pl.when(lax.rem(j, X) != x)
+        def _():
+            for part in range(2):
+                kv(part, j, me, 0).wait_recv()
+            arrive(j)
+
+    loop(plane, me, from_across)
+    loop(1, me // X + 1, from_column)
+    loop(1, plane + 1, lambda i: from_across(plane - i))
 
     for g in range(KV):
         total = tot[g]
@@ -182,7 +229,7 @@
             cols = slice(g * HEAD, (g + 1) * HEAD)
             key = kall[j, :, cols]
             s = nt(key, qs[g]) * c2
-            dp = nt(vall[j, :, cols], dos[g])
+            dp = nt(vval[j, :, cols], dos[g])
             if first:
                 s = jnp.where(seen, s, NEG)
             p = jnp.exp2(s - top[g])
@@ -284,12 +331,13 @@
         sigma[:, cols] = value * noise[:, cols]
 
     def drain_later(who):
-        k_copy(who).wait_send()
-        v_copy(who).wait_send()
         l_copy(who).wait_send()
 
     loop(me + 1, n, drain_later)
     loop(0, me, lambda j: g_copy(j).wait_send())
+    for part in range(2):
+        hand_on(me, part, True, lambda c: c.wait_send())
+        loop(1, me // X + 1, lambda i: hand_on(me - i * X, part, False, lambda c: c.wait_send()))
 
     def drain_tp(d):
         who = lax.rem(t + d, m)
@@ -304,6 +352,18 @@
         a_copy(who).wait_send()
 
     loop(1, n, drain_seq)
+
+
+def hand_out(*refs):
+    count = (len(refs) - 1) // 2
+    sems = refs[-1]
+    copies = [
+        pltpu.make_async_copy(refs[i], refs[count + i], sems.at[i]) for i in range(count)
+    ]
+    for c in copies:
+        c.start()
+    for c in copies:
+        c.wait()
 
 
 def solution(mesh):
@@ -319,14 +379,19 @@
         units = (2 * DL + QL + KL) // HEAD
         per = -(-units // n)
         shape = lambda cols: jax.ShapeDtypeStruct((RANK, cols), F32)
+        X = 1
+        while 2 * (2 * X) ** 2 <= n:
+            X *= 2
+        hbm = pl.BlockSpec(memory_space=pltpu.HBM)
         vmem = pl.BlockSpec(memory_space=pltpu.VMEM)
         sem = pltpu.SemaphoreType.DMA
-        return tuple(pl.pallas_call(
-            functools.partial(kernel, n, m, units, per),
+        outs = pl.pallas_call(
+            functools.partial(kernel, n, m, units, per, X),
             out_shape=[shape(c) for c in (DL, DL, QL, QL, DL, DL, KL, KL)],
-            in_specs=[vmem] * 17,
+            in_specs=[hbm] * 17,
             out_specs=[vmem] * 8,
-            scratch_shapes=[
+            scratch_shapes=[pltpu.VMEM(a.shape, a.dtype) for a in args] + [
+                pltpu.VMEM((n, T, KL), BF16),
                 pltpu.VMEM((n, T, KL), BF16),
                 pltpu.VMEM((n, T, KL), BF16),
                 pltpu.VMEM((n, RANK, T), BF16),
@@ -345,16 +410,25 @@
                 pltpu.VMEM((n, per, RANK, HEAD), BF16),
                 pltpu.VMEM((n, per, RANK, HEAD), BF16),
                 pltpu.VMEM((n, per, RANK, HEAD), BF16),
-            ] + [sem((k,)) for k in (n, n, n, n, n, n, m, m, m, m, n, n, n, n, n, n)],
+            ] + [sem((n, 1 + X)), sem((n,)), sem((n, 1 + X)), sem((n,))]
+            + [sem((k,)) for k in (n, n, m, m, m, m, n, n, n, n, n, n, 17)],
             compiler_params=pltpu.CompilerParams(
-                collective_id=0, has_side_effects=True, vmem_limit_bytes=48 * 1024 * 1024
+                collective_id=0, has_side_effects=True, vmem_limit_bytes=63 * 1024 * 1024
             ),
             cost_estimate=pl.CostEstimate(
                 flops=14 * rows * KV * n * T * HEAD // 2,
                 bytes_accessed=8 * 1024 * 1024,
                 transcendentals=rows * KV * n * T,
             ),
-        )(*args))
+        )(*args)
+        return tuple(pl.pallas_call(
+            hand_out,
+            out_shape=[jax.ShapeDtypeStruct(a.shape, a.dtype) for a in outs],
+            in_specs=[hbm] * 8,
+            out_specs=[hbm] * 8,
+            scratch_shapes=[sem((8,))],
+            compiler_params=pltpu.CompilerParams(vmem_limit_bytes=63 * 1024 * 1024),
+        )(*outs))
 
     wide = P("seq", "tp")
     flat = P(None, "tp")

time: 113 us -> 89 us (0.79)
  local copies, waits for them, and re-layouts: 20.3 us -> 0 us
  Pallas kernels: 91.3 us -> 88.2 us
    unnamed x42 -> x0, local copies, waits for them, and re-layouts: 20.3 us -> none
    pallas_call x1 -> x2, Pallas kernels: 91.3 us -> 88.2 us  [the longest x1 66.2 us: step(): pl.pallas_call(functools.partial(kernel, n, m, units, per, X), out_shape=...]
where the time goes in v2:
time: 89 us; the launch traced here: 88.8 us
  Pallas kernels  88.2 us (99%)
    pallas_call x1, Pallas kernels, step(): pl.pallas_call(functools.partial(kernel, n, m, units, per, X), out_shape=...  66.2 us
    pallas_call x1, Pallas kernels, step(): pl.pallas_call(hand_out, out_shape=[jax.ShapeDtypeStruct(a.shape, a.dtype...  22 us

profile of v2, /device:TPU:0, one launch (start us, length us, event | category | flops | bytes accessed | tf_op | source)
XLA Modules:
  0.0 88.8 jit_solution(2703321265153947288)
XLA Ops:
  0.6 66.2 %shard_map.224 = (f32[16,2048]{1,0:T(8,128)}, f32[16,2048]{1,0:T(8,128)}, f32[16,1024]{1,0:T(8,128)}, f32[16,1024]{1,0:T(8,128)}, f32[16,2048]{1,0:T(8,128)}, /*...) custom-call(bf16[256,2048]{1,0:T(8,128)(2,1)} %refs_0_.1, bf16[256,1024]{1,0:T(8,128)(2,1)} %refs_1_.1, ...), custom_call_target="tpu_custom_call" | custom-call | flops 3758096384 | bytes 8388608 | tf_op jit(solution)/shard_map/pallas_call | solution.py:388
  66.8 22.0 %shard_map.225 = (f32[16,2048]{1,0:T(8,128)}, f32[16,2048]{1,0:T(8,128)}, f32[16,1024]{1,0:T(8,128)}, f32[16,1024]{1,0:T(8,128)}, f32[16,2048]{1,0:T(8,128)}, /*...) custom-call(f32[16,2048]{1,0:T(8,128)} %get-tuple-element.16.refs_0_, ...), custom_call_target="tpu_custom_call" | custom-call | tf_op jit(solution)/shard_map/pallas_call | solution.py:424

commit v3 on v2

--- a/solution.py
+++ b/solution.py
@@ -29,20 +29,18 @@
 
 
 def kernel(
-    n, m, units, per, X, *refs,
+    n, m, up_per, down_per, keep, X, *refs,
 ):
     sources = refs[:17]
-    held = refs[25:42]
+    held = refs[19:36]
     loaded = refs[-1]
     hidden, qbase, kc, vb, og, qdm, qds, qdn, qum, qus, qun, vdm, vds, vdn, vum, vus, vun = held
     kc, vb = sources[2:4]
+    up_out, down_out = refs[17:19]
     (
-        o_qd, o_qds, o_qu, o_qus, o_vd, o_vds, o_vu, o_vus,
-    ) = refs[17:25]
-    (
-    kall, vall, vval, vlow_all, lowx, gx, qs, dos, top, tot, wei, dqt, vgs, vgx, vug, quw, pack, rsx, agx,
-    k_s, k_r, v_s, v_r, l_s, l_r, x_s, x_r, y_s, y_r, g_s, g_r, r_s, r_r, a_s, a_r,
-    ) = refs[42:-1]
+    kall, vall, vval, vlow_all, lowx, gx, qs, dos, top, tot, wei, dqt, vgs, vgx, vug, quw, up_pack, up_rsx, up_agx, down_pack, down_rsx, down_agx, s_kept, dp_kept,
+    k_s, k_r, v_s, v_r, l_s, l_r, x_s, x_r, y_s, y_r, g_s, g_r, ur_s, ur_r, ua_s, ua_r, dr_s, dr_r, da_s, da_r,
+    ) = refs[36:-1]
     T, DL = hidden.shape
     KV = kc.shape[1] // HEAD
     rows = GROUP * T
@@ -179,6 +177,10 @@
             dp = nt(vval[j, :, cols], dos[g])
             if first:
                 s = jnp.where(seen, s, NEG)
+            if keep:
+                s_kept[j, g] = s
+                dp_kept[j, g] = dp
+            if first:
                 new = jnp.max(s, axis=0, keepdims=True)
                 e = jnp.exp2(s - new)
                 tot[g] = jnp.sum(e, axis=0, keepdims=True)
@@ -223,40 +225,39 @@
         top[g] = top[g] + jnp.log2(total)
         wei[g] = wei[g] / total
 
-    def grads(j, first):
+    dqt[...] = jnp.zeros_like(dqt)
+    vug[...] = jnp.zeros_like(vug)
+
+    def grads(j, own):
         part = jnp.zeros((RANK, T), F32)
         for g in range(KV):
             cols = slice(g * HEAD, (g + 1) * HEAD)
             key = kall[j, :, cols]
-            s = nt(key, qs[g]) * c2
-            dp = nt(vval[j, :, cols], dos[g])
-            if first:
-                s = jnp.where(seen, s, NEG)
+            if keep:
+                s = s_kept[j, g]
+                dp = dp_kept[j, g]
+            else:
+                s = nt(key, qs[g]) * c2
+                dp = nt(vval[j, :, cols], dos[g])
+                if own:
+                    s = jnp.where(seen, s, NEG)
             p = jnp.exp2(s - top[g])
             ds = (p * (dp - wei[g])).astype(BF16)
-            dq = tn(key, ds)
+            dqt[g] += tn(key, ds)
             dv = nn(p.astype(BF16), dos[g]).astype(BF16)
             part = part + nt(vup[:, cols], dv)
-            vu = nn(vlow_all[j], dv)
-            if first:
-                dqt[g] = dq
-                vug[g] = vu
-            else:
-                dqt[g] += dq
-                vug[g] += vu
+            vug[g] += nn(vlow_all[j], dv)
         vgs[j] = part
-
-    grads(me, True)
 
     def g_copy(j):
         return to_seq(vgs.at[j], vgx.at[me], g_s.at[j], g_r.at[me], j)
 
-    def grads_step(i):
-        j = me - i
+    def grads_step(j):
         grads(j, False)
         g_copy(j).start()
 
-    loop(1, me + 1, grads_step)
+    loop(0, me, grads_step)
+    grads(me, True)
 
     qg = jnp.zeros((RANK, T), F32)
     for g in range(KV):
@@ -266,6 +267,38 @@
             qg = qg + nn(qup[:, at:at + HEAD], dq)
             quw[:, at:at + HEAD] = nt(qlow, dq)
 
+    def deal(tiles, per, pack):
+        for i in range(n * per):
+            pack[i // per, i % per] = (
+                tiles[i].astype(BF16) if i < len(tiles) else jnp.zeros((RANK, HEAD), BF16)
+            )
+
+    def others(act):
+        loop(1, n, lambda d: act(lax.rem(me + d, n)))
+
+    def r_copy(pack, rsx, ss, rs, who):
+        return to_seq(pack.at[who], rsx.at[me], ss.at[who], rs.at[me], who)
+
+    def a_copy(agx, ss, rs, who):
+        return to_seq(agx.at[me], agx.at[me], ss.at[who], rs.at[me], who)
+
+    def reduce_in(pack, rsx, agx, ss, rs):
+        rsx[me] = pack[me]
+        others(lambda w: to_seq(pack.at[w], rsx.at[w], ss.at[w], rs.at[w], w).wait_recv())
+        total = rsx[0].astype(F32)
+        for i in range(1, n):
+            total = total + rsx[i].astype(F32)
+        agx[me] = total.astype(BF16)
+
+    def gather_in(agx, ss, rs):
+        others(lambda w: to_seq(agx.at[w], agx.at[w], ss.at[w], rs.at[w], w).wait_recv())
+
+    deal(
+        [quw[:, k * HEAD:(k + 1) * HEAD] for k in range(KV * GROUP)] + [vug[k] for k in range(KV)],
+        up_per, up_pack,
+    )
+    others(lambda w: r_copy(up_pack, up_rsx, ur_s, ur_r, w).start())
+
     def g_in(src):
         to_seq(vgs.at[src], vgx.at[src], g_s.at[src], g_r.at[src], src).wait_recv()
 
@@ -286,49 +319,20 @@
         lg = lg + gx[i]
     dg = nn(lg.astype(BF16), hidden[...])
 
-    outs = []
-    for k in range(DL // HEAD):
-        outs.append((dg[:RANK, k * HEAD:(k + 1) * HEAD], o_qd, o_qds, qdn, k))
-    for k in range(DL // HEAD):
-        outs.append((dg[RANK:, k * HEAD:(k + 1) * HEAD], o_vd, o_vds, vdn, k))
-    for k in range(KV * GROUP):
-        outs.append((quw[:, k * HEAD:(k + 1) * HEAD], o_qu, o_qus, qun, k))
-    for k in range(KV):
-        outs.append((vug[k], o_vu, o_vus, vun, k))
-    for i in range(n * per):
-        if i < units:
-            pack[i // per, i % per] = outs[i][0].astype(BF16)
-        else:
-            pack[i // per, i % per] = jnp.zeros((RANK, HEAD), BF16)
-
-    def r_copy(who):
-        return to_seq(pack.at[who], rsx.at[me], r_s.at[who], r_r.at[me], who)
-
-    def r_in(src):
-        return to_seq(pack.at[src], rsx.at[src], r_s.at[src], r_r.at[src], src)
-
-    loop(1, n, lambda d: r_copy(lax.rem(me + d, n)).start())
-    rsx[me] = pack[me]
-    loop(1, n, lambda d: r_in(lax.rem(me + d, n)).wait_recv())
-    total = rsx[0].astype(F32)
-    for i in range(1, n):
-        total = total + rsx[i].astype(F32)
-    agx[me] = total.astype(BF16)
-
-    def a_copy(who):
-        return to_seq(agx.at[me], agx.at[me], a_s.at[who], a_r.at[me], who)
-
-    def a_in(src):
-        return to_seq(agx.at[src], agx.at[src], a_s.at[src], a_r.at[src], src)
-
-    loop(1, n, lambda d: a_copy(lax.rem(me + d, n)).start())
-    loop(1, n, lambda d: a_in(lax.rem(me + d, n)).wait_recv())
-    for i in range(units):
-        _, mean, sigma, noise, k = outs[i]
-        cols = slice(k * HEAD, (k + 1) * HEAD)
-        value = agx[i // per, i % per].astype(F32)
-        mean[:, cols] = value
-        sigma[:, cols] = value * noise[:, cols]
+    deal(
+        [dg[:RANK, k * HEAD:(k + 1) * HEAD] for k in range(DL // HEAD)]
+        + [dg[RANK:, k * HEAD:(k + 1) * HEAD] for k in range(DL // HEAD)],
+        down_per, down_pack,
+    )
+    others(lambda w: r_copy(down_pack, down_rsx, dr_s, dr_r, w).start())
+    reduce_in(up_pack, up_rsx, up_agx, ur_s, ur_r)
+    others(lambda w: a_copy(up_agx, ua_s, ua_r, w).start())
+    reduce_in(down_pack, down_rsx, down_agx, dr_s, dr_r)
+    others(lambda w: a_copy(down_agx, da_s, da_r, w).start())
+    gather_in(up_agx, ua_s, ua_r)
+    up_out[...] = up_agx[...]
+    gather_in(down_agx, da_s, da_r)
+    down_out[...] = down_agx[...]
 
     def drain_later(who):
         l_copy(who).wait_send()
@@ -348,21 +352,42 @@
 
     def drain_seq(d):
         who = lax.rem(me + d, n)
-        r_copy(who).wait_send()
-        a_copy(who).wait_send()
+        r_copy(up_pack, up_rsx, ur_s, ur_r, who).wait_send()
+        a_copy(up_agx, ua_s, ua_r, who).wait_send()
+        r_copy(down_pack, down_rsx, dr_s, dr_r, who).wait_send()
+        a_copy(down_agx, da_s, da_r, who).wait_send()
 
     loop(1, n, drain_seq)
 
 
 def hand_out(*refs):
-    count = (len(refs) - 1) // 2
-    sems = refs[-1]
-    copies = [
-        pltpu.make_async_copy(refs[i], refs[count + i], sems.at[i]) for i in range(count)
+    up, down = refs[6 + 8:6 + 8 + 2]
+    noises = refs[16:20]
+    outs = refs[20:28]
+    in_sem, out_sem = refs[28:]
+    loads = [
+        pltpu.make_async_copy(refs[i], refs[14 + i], in_sem.at[i]) for i in range(6)
     ]
-    for c in copies:
+    stores = [
+        pltpu.make_async_copy(outs[i], refs[6 + i], out_sem.at[i]) for i in range(8)
+    ]
+    for c in loads:
         c.start()
-    for c in copies:
+    for c in loads:
+        c.wait()
+    per = (up.shape[1], down.shape[1])
+    at = [0, 0]
+    for which, i in ((1, 0), (1, 2), (0, 1), (0, 3)):
+        for k in range(noises[i].shape[1] // HEAD):
+            unit = at[which]
+            at[which] += 1
+            cols = slice(k * HEAD, (k + 1) * HEAD)
+            value = (up, down)[which][unit // per[which], unit % per[which]].astype(F32)
+            outs[2 * i][:, cols] = value
+            outs[2 * i + 1][:, cols] = value * noises[i][:, cols]
+        stores[2 * i].start()
+        stores[2 * i + 1].start()
+    for c in stores:
         c.wait()
 
 
@@ -376,8 +401,10 @@
         QL, KL = qbase.shape[1], kc.shape[1]
         KV = KL // HEAD
         rows = GROUP * T
-        units = (2 * DL + QL + KL) // HEAD
-        per = -(-units // n)
+        up_per = -(-(QL + KL) // (HEAD * n))
+        down_per = -(-2 * DL // (HEAD * n))
+        keep = n * KV * T * rows * 8 <= 36 * 1024 * 1024
+        kept = (n, KV, T, rows) if keep else (1, 1, 8, HEAD)
         shape = lambda cols: jax.ShapeDtypeStruct((RANK, cols), F32)
         X = 1
         while 2 * (2 * X) ** 2 <= n:
@@ -386,10 +413,13 @@
         vmem = pl.BlockSpec(memory_space=pltpu.VMEM)
         sem = pltpu.SemaphoreType.DMA
         outs = pl.pallas_call(
-            functools.partial(kernel, n, m, units, per, X),
-            out_shape=[shape(c) for c in (DL, DL, QL, QL, DL, DL, KL, KL)],
+            functools.partial(kernel, n, m, up_per, down_per, keep, X),
+            out_shape=[
+                jax.ShapeDtypeStruct((n, up_per, RANK, HEAD), BF16),
+                jax.ShapeDtypeStruct((n, down_per, RANK, HEAD), BF16),
+            ],
             in_specs=[hbm] * 17,
-            out_specs=[vmem] * 8,
+            out_specs=[vmem] * 2,
             scratch_shapes=[pltpu.VMEM(a.shape, a.dtype) for a in args] + [
                 pltpu.VMEM((n, T, KL), BF16),
                 pltpu.VMEM((n, T, KL), BF16),
@@ -407,11 +437,12 @@
                 pltpu.VMEM((n, RANK, T), F32),
                 pltpu.VMEM((KV, RANK, HEAD), F32),
                 pltpu.VMEM((RANK, QL), F32),
-                pltpu.VMEM((n, per, RANK, HEAD), BF16),
-                pltpu.VMEM((n, per, RANK, HEAD), BF16),
-                pltpu.VMEM((n, per, RANK, HEAD), BF16),
+            ] + [pltpu.VMEM((n, up_per, RANK, HEAD), BF16)] * 3
+            + [pltpu.VMEM((n, down_per, RANK, HEAD), BF16)] * 3 + [
+                pltpu.VMEM(kept, F32),
+                pltpu.VMEM(kept, F32),
             ] + [sem((n, 1 + X)), sem((n,)), sem((n, 1 + X)), sem((n,))]
-            + [sem((k,)) for k in (n, n, m, m, m, m, n, n, n, n, n, n, 17)],
+            + [sem((k,)) for k in (n, n, m, m, m, m) + (n,) * 10 + (17,)],
             compiler_params=pltpu.CompilerParams(
                 collective_id=0, has_side_effects=True, vmem_limit_bytes=63 * 1024 * 1024
             ),
@@ -421,14 +452,17 @@
                 transcendentals=rows * KV * n * T,
             ),
         )(*args)
+        taken = tuple(outs) + (args[7], args[10], args[13], args[16])
+        results = [shape(c) for c in (DL, DL, QL, QL, DL, DL, KL, KL)]
         return tuple(pl.pallas_call(
             hand_out,
-            out_shape=[jax.ShapeDtypeStruct(a.shape, a.dtype) for a in outs],
-            in_specs=[hbm] * 8,
+            out_shape=results,
+            in_specs=[hbm] * 6,
             out_specs=[hbm] * 8,
-            scratch_shapes=[sem((8,))],
+            scratch_shapes=[pltpu.VMEM(a.shape, a.dtype) for a in taken + tuple(results)]
+            + [sem((6,)), sem((8,))],
             compiler_params=pltpu.CompilerParams(vmem_limit_bytes=63 * 1024 * 1024),
-        )(*outs))
+        )(*taken))
 
     wide = P("seq", "tp")
     flat = P(None, "tp")

time: 89 us -> 60.3 us (0.68)
  Pallas kernels: 88.2 us -> 59.5 us
    pallas_call x2, Pallas kernels: 88.2 us -> 59.5 us  [the longest x1 57.4 us: step(): pl.pallas_call(functools.partial(kernel, n, m, up_per, down_per, keep, X)...]
where the time goes in v3:
time: 60.3 us; the launch traced here: 60.2 us
  Pallas kernels  59.5 us (99%)
  between operations  0.65 us (1%)
    pallas_call x1, Pallas kernels, step(): pl.pallas_call(functools.partial(kernel, n, m, up_per, down_per, keep, X)...  57.4 us
    pallas_call x1, Pallas kernels, step(): pl.pallas_call(hand_out, out_shape=results, in_specs=[hbm] * 6, out_specs...  2.07 us

profile of v3, /device:TPU:0, one launch (start us, length us, event | category | flops | bytes accessed | tf_op | source)
XLA Modules:
  0.0 60.2 jit_solution(14654301441772905938)
XLA Ops:
  0.6 57.4 %shard_map.224 = (bf16[8,2,16,128]{3,2,1,0:T(8,128)(2,1)}, bf16[8,4,16,128]{3,2,1,0:T(8,128)(2,1)}) custom-call(bf16[256,2048]{1,0:T(8,128)(2,1)} %refs_0_.1, bf16[256,1024]{1,0:T(8,128)(2,1)} %refs_1_.1, bf16[256,256]{1,0:T(8,128)(2,1)} %refs_2_.2, bf16[256,256]{1,0:T(8,128)(2,1)} %refs_3_.2, bf16[256,1024]{1,0:T(8,128)(2,1)} %refs_4_.2, ...), custom_call_target="tpu_custom_call" | custom-call | flops 3758096384 | bytes 8388608 | tf_op jit(solution)/shard_map/pallas_call | solution.py:415
  58.1 2.1 %shard_map.225 = (f32[16,2048]{1,0:T(8,128)}, f32[16,2048]{1,0:T(8,128)}, f32[16,1024]{1,0:T(8,128)}, f32[16,1024]{1,0:T(8,128)}, f32[16,2048]{1,0:T(8,128)}, /*...) custom-call(bf16[8,2,16,128]{3,2,1,0:T(8,128)(2,1)} %get-tuple-element.10.refs_0_, ...), custom_call_target="tpu_custom_call" | custom-call | tf_op jit(solution)/shard_map/pallas_call | solution.py:457

commit v4 on v3

--- a/solution.py
+++ b/solution.py
@@ -119,8 +119,7 @@
 
         loop(1, X, across)
 
-    for part in range(2):
-        hand_on(me, part, True, lambda c: c.start())
+    hand_on(me, 0, True, lambda c: c.start())
 
     for i in order[:7]:
         load(i).wait()
@@ -143,6 +142,15 @@
         for h in range(GROUP):
             at = (g * GROUP + h) * HEAD
             dos[g, h * T:(h + 1) * T, :] = og[:, at:at + HEAD]
+
+    def key_on(j):
+        kv(0, j, me, 0).wait_recv()
+        hand_on(j, 0, False, lambda c: c.start())
+
+    @pl.when(me >= X)
+    def _():
+        key_on(me - X)
+
     loop(1, m, lambda d: x_in(lax.rem(t + d, m)).wait_recv())
     low = lowx[0]
     for i in range(1, m):
@@ -170,94 +178,106 @@
     def make_value(j):
         vval[j] = (vall[j].astype(F32) + tn(vlow_all[j], vup)).astype(BF16)
 
-    def stats(j, first):
+    def scores(j, g, own):
+        s = nt(kall[j, :, g * HEAD:(g + 1) * HEAD], qs[g]) * c2
+        return jnp.where(seen, s, NEG) if own else s
+
+    def stats(j, own):
         for g in range(KV):
-            cols = slice(g * HEAD, (g + 1) * HEAD)
-            s = nt(kall[j, :, cols], qs[g]) * c2
-            dp = nt(vval[j, :, cols], dos[g])
-            if first:
-                s = jnp.where(seen, s, NEG)
+            s = scores(j, g, own)
             if keep:
                 s_kept[j, g] = s
-                dp_kept[j, g] = dp
-            if first:
-                new = jnp.max(s, axis=0, keepdims=True)
-                e = jnp.exp2(s - new)
-                tot[g] = jnp.sum(e, axis=0, keepdims=True)
-                wei[g] = jnp.sum(e * dp, axis=0, keepdims=True)
+            new = jnp.max(s, axis=0, keepdims=True)
+            if own:
+                tot[g] = jnp.sum(jnp.exp2(s - new), axis=0, keepdims=True)
             else:
                 old = top[g]
-                new = jnp.maximum(old, jnp.max(s, axis=0, keepdims=True))
-                e = jnp.exp2(s - new)
-                decay = jnp.exp2(old - new)
-                tot[g] = tot[g] * decay + jnp.sum(e, axis=0, keepdims=True)
-                wei[g] = wei[g] * decay + jnp.sum(e * dp, axis=0, keepdims=True)
+                new = jnp.maximum(old, new)
+                tot[g] = tot[g] * jnp.exp2(old - new) + jnp.sum(
+                    jnp.exp2(s - new), axis=0, keepdims=True
+                )
             top[g] = new
 
-    make_value(me)
     stats(me, True)
 
-    def arrive(j):
-        to_seq(vlow_all.at[j], vlow_all.at[j], l_s.at[j], l_r.at[j], j).wait_recv()
-        make_value(j)
+    def key_column(i):
+        j = me - i * X
+
+        @pl.when(i > 1)
+        def _():
+            key_on(j)
+
         stats(j, False)
 
-    def from_column(i):
-        j = me - i * X
-        for part in range(2):
-            kv(part, j, me, 0).wait_recv()
-            hand_on(j, part, False, lambda c: c.start())
-        arrive(j)
-
-    def from_across(j):
-        @pl.when(lax.rem(j, X) != x)
-        def _():
-            for part in range(2):
+    def across(part, act):
+        def visit(j):
+            @pl.when(lax.rem(j, X) != x)
+            def _():
                 kv(part, j, me, 0).wait_recv()
-            arrive(j)
-
-    loop(plane, me, from_across)
-    loop(1, me // X + 1, from_column)
-    loop(1, plane + 1, lambda i: from_across(plane - i))
+                act(j, False)
+
+        loop(plane, me, visit)
+        loop(1, plane + 1, lambda i: visit(plane - i))
+
+    loop(1, me // X + 1, key_column)
+    hand_on(me, 1, True, lambda c: c.start())
+    across(0, stats)
 
     for g in range(KV):
-        total = tot[g]
-        top[g] = top[g] + jnp.log2(total)
-        wei[g] = wei[g] / total
-
+        top[g] = top[g] + jnp.log2(tot[g])
     dqt[...] = jnp.zeros_like(dqt)
     vug[...] = jnp.zeros_like(vug)
-
-    def grads(j, own):
+    wei[...] = jnp.zeros_like(wei)
+
+    def g_copy(j):
+        return to_seq(vgs.at[j], vgx.at[me], g_s.at[j], g_r.at[me], j)
+
+    def weigh(j, own):
+        make_value(j)
         part = jnp.zeros((RANK, T), F32)
         for g in range(KV):
             cols = slice(g * HEAD, (g + 1) * HEAD)
-            key = kall[j, :, cols]
+            p = jnp.exp2((s_kept[j, g] if keep else scores(j, g, own)) - top[g])
+            dp = nt(vval[j, :, cols], dos[g])
             if keep:
-                s = s_kept[j, g]
-                dp = dp_kept[j, g]
-            else:
-                s = nt(key, qs[g]) * c2
-                dp = nt(vval[j, :, cols], dos[g])
-                if own:
-                    s = jnp.where(seen, s, NEG)
-            p = jnp.exp2(s - top[g])
-            ds = (p * (dp - wei[g])).astype(BF16)
-            dqt[g] += tn(key, ds)
+                s_kept[j, g] = p
+                dp_kept[j, g] = dp
+            wei[g] += jnp.sum(p * dp, axis=0, keepdims=True)
             dv = nn(p.astype(BF16), dos[g]).astype(BF16)
             part = part + nt(vup[:, cols], dv)
             vug[g] += nn(vlow_all[j], dv)
         vgs[j] = part
 
-    def g_copy(j):
-        return to_seq(vgs.at[j], vgx.at[me], g_s.at[j], g_r.at[me], j)
-
-    def grads_step(j):
-        grads(j, False)
+    def weigh_other(j, own):
+        to_seq(vlow_all.at[j], vlow_all.at[j], l_s.at[j], l_r.at[j], j).wait_recv()
+        weigh(j, own)
         g_copy(j).start()
 
-    loop(0, me, grads_step)
-    grads(me, True)
+    weigh(me, True)
+
+    def value_column(i):
+        j = me - i * X
+        kv(1, j, me, 0).wait_recv()
+        hand_on(j, 1, False, lambda c: c.start())
+        weigh_other(j, False)
+
+    loop(1, me // X + 1, value_column)
+    across(1, weigh_other)
+
+    def turn(j, own):
+        for g in range(KV):
+            cols = slice(g * HEAD, (g + 1) * HEAD)
+            if keep:
+                p = s_kept[j, g]
+                dp = dp_kept[j, g]
+            else:
+                p = jnp.exp2(scores(j, g, own) - top[g])
+                dp = nt(vval[j, :, cols], dos[g])
+            ds = (p * (dp - wei[g])).astype(BF16)
+            dqt[g] += tn(kall[j, :, cols], ds)
+
+    loop(0, me, lambda j: turn(j, False))
+    turn(me, True)
 
     qg = jnp.zeros((RANK, T), F32)
     for g in range(KV):

time: 60.3 us -> 59.1 us (0.980)
  Pallas kernels: 59.5 us -> 58.3 us
    pallas_call x1, Pallas kernels: 57.4 us -> 56.2 us  [step(): pl.pallas_call(functools.partial(kernel, n, m, up_per, down_per, keep, X)...]
where the time goes in v4:
time: 59.1 us; the launch traced here: 59 us
  Pallas kernels  58.3 us (99%)
  between operations  0.65 us (1%)
    pallas_call x1, Pallas kernels, step(): pl.pallas_call(functools.partial(kernel, n, m, up_per, down_per, keep, X)...  56.2 us
    pallas_call x1, Pallas kernels, step(): pl.pallas_call(hand_out, out_shape=results, in_specs=[hbm] * 6, out_specs...  2.07 us

profile of v4, /device:TPU:0, one launch (start us, length us, event | category | flops | bytes accessed | tf_op | source)
XLA Modules:
  0.0 59.0 jit_solution(2484072663955998853)
XLA Ops:
  0.6 56.2 %shard_map.224 = (bf16[8,2,16,128]{3,2,1,0:T(8,128)(2,1)}, bf16[8,4,16,128]{3,2,1,0:T(8,128)(2,1)}) custom-call(bf16[256,2048]{1,0:T(8,128)(2,1)} %refs_0_.1, bf16[256,1024]{1,0:T(8,128)(2,1)} %refs_1_.1, bf16[256,256]{1,0:T(8,128)(2,1)} %refs_2_.2, bf16[256,256]{1,0:T(8,128)(2,1)} %refs_3_.2, bf16[256,1024]{1,0:T(8,128)(2,1)} %refs_4_.2, ...), custom_call_target="tpu_custom_call" | custom-call | flops 3758096384 | bytes 8388608 | tf_op jit(solution)/shard_map/pallas_call | solution.py:435
  56.9 2.1 %shard_map.225 = (f32[16,2048]{1,0:T(8,128)}, f32[16,2048]{1,0:T(8,128)}, f32[16,1024]{1,0:T(8,128)}, f32[16,1024]{1,0:T(8,128)}, f32[16,2048]{1,0:T(8,128)}, /*...) custom-call(bf16[8,2,16,128]{3,2,1,0:T(8,128)(2,1)} %get-tuple-element.10.refs_0_, ...), custom_call_target="tpu_custom_call" | custom-call | tf_op jit(solution)/shard_map/pallas_call | solution.py:477

commit v5 on v4

--- a/solution.py
+++ b/solution.py
@@ -171,32 +171,34 @@
             q = qbase[:, at:at + HEAD].astype(F32) + tn(qlow, qup[:, at:at + HEAD])
             qs[g, h * T:(h + 1) * T, :] = q.astype(BF16)
 
-    key_pos = lax.broadcasted_iota(jnp.int32, (T, rows), 0)
-    row_pos = lax.broadcasted_iota(jnp.int32, (T, rows), 1) % T
+    key_pos = lax.broadcasted_iota(jnp.int32, (T, T), 0)
+    row_pos = lax.broadcasted_iota(jnp.int32, (T, T), 1)
     seen = key_pos <= row_pos
 
     def make_value(j):
         vval[j] = (vall[j].astype(F32) + tn(vlow_all[j], vup)).astype(BF16)
 
-    def scores(j, g, own):
-        s = nt(kall[j, :, g * HEAD:(g + 1) * HEAD], qs[g]) * c2
+    heads = [slice(h * T, (h + 1) * T) for h in range(GROUP)]
+
+    def scores(j, g, r, own):
+        s = nt(kall[j, :, g * HEAD:(g + 1) * HEAD], qs[g, r, :]) * c2
         return jnp.where(seen, s, NEG) if own else s
 
     def stats(j, own):
-        for g in range(KV):
-            s = scores(j, g, own)
+        for g, r in [(g, r) for g in range(KV) for r in heads]:
+            s = scores(j, g, r, own)
             if keep:
-                s_kept[j, g] = s
+                s_kept[j, g, :, r] = s
             new = jnp.max(s, axis=0, keepdims=True)
             if own:
-                tot[g] = jnp.sum(jnp.exp2(s - new), axis=0, keepdims=True)
+                tot[g, :, r] = jnp.sum(jnp.exp2(s - new), axis=0, keepdims=True)
             else:
-                old = top[g]
+                old = top[g, :, r]
                 new = jnp.maximum(old, new)
-                tot[g] = tot[g] * jnp.exp2(old - new) + jnp.sum(
+                tot[g, :, r] = tot[g, :, r] * jnp.exp2(old - new) + jnp.sum(
                     jnp.exp2(s - new), axis=0, keepdims=True
                 )
-            top[g] = new
+            top[g, :, r] = new
 
     stats(me, True)
 
@@ -237,13 +239,16 @@
         part = jnp.zeros((RANK, T), F32)
         for g in range(KV):
             cols = slice(g * HEAD, (g + 1) * HEAD)
-            p = jnp.exp2((s_kept[j, g] if keep else scores(j, g, own)) - top[g])
-            dp = nt(vval[j, :, cols], dos[g])
-            if keep:
-                s_kept[j, g] = p
-                dp_kept[j, g] = dp
-            wei[g] += jnp.sum(p * dp, axis=0, keepdims=True)
-            dv = nn(p.astype(BF16), dos[g]).astype(BF16)
+            dv = jnp.zeros((T, HEAD), F32)
+            for r in heads:
+                p = jnp.exp2((s_kept[j, g, :, r] if keep else scores(j, g, r, own)) - top[g, :, r])
+                dp = nt(vval[j, :, cols], dos[g, r, :])
+                if keep:
+                    s_kept[j, g, :, r] = p
+                    dp_kept[j, g, :, r] = dp
+                wei[g, :, r] += jnp.sum(p * dp, axis=0, keepdims=True)
+                dv = dv + nn(p.astype(BF16), dos[g, r, :])
+            dv = dv.astype(BF16)
             part = part + nt(vup[:, cols], dv)
             vug[g] += nn(vlow_all[j], dv)
         vgs[j] = part
@@ -267,14 +272,15 @@
     def turn(j, own):
         for g in range(KV):
             cols = slice(g * HEAD, (g + 1) * HEAD)
-            if keep:
-                p = s_kept[j, g]
-                dp = dp_kept[j, g]
-            else:
-                p = jnp.exp2(scores(j, g, own) - top[g])
-                dp = nt(vval[j, :, cols], dos[g])
-            ds = (p * (dp - wei[g])).astype(BF16)
-            dqt[g] += tn(kall[j, :, cols], ds)
+            for r in heads:
+                if keep:
+                    p = s_kept[j, g, :, r]
+                    dp = dp_kept[j, g, :, r]
+                else:
+                    p = jnp.exp2(scores(j, g, r, own) - top[g, :, r])
+                    dp = nt(vval[j, :, cols], dos[g, r, :])
+                ds = (p * (dp - wei[g, :, r])).astype(BF16)
+                dqt[g, :, r] += tn(kall[j, :, cols], ds)
 
     loop(0, me, lambda j: turn(j, False))
     turn(me, True)

time: 59.1 us -> 59.1 us (level)
  no operation moved by 1% of the time
where the time goes in v5:
time: 59.1 us; the launch traced here: 58.9 us
  Pallas kernels  58.3 us (99%)
  between operations  0.65 us (1%)
    pallas_call x1, Pallas kernels, step(): pl.pallas_call(functools.partial(kernel, n, m, up_per, down_per, keep, X)...  56.2 us
    pallas_call x1, Pallas kernels, step(): pl.pallas_call(hand_out, out_shape=results, in_specs=[hbm] * 6, out_specs...  2.07 us

profile of v5, /device:TPU:0, one launch (start us, length us, event | category | flops | bytes accessed | tf_op | source)
XLA Modules:
  0.0 58.9 jit_solution(7289793131611626571)
XLA Ops:
  0.6 56.2 %shard_map.224 = (bf16[8,2,16,128]{3,2,1,0:T(8,128)(2,1)}, bf16[8,4,16,128]{3,2,1,0:T(8,128)(2,1)}) custom-call(bf16[256,2048]{1,0:T(8,128)(2,1)} %refs_0_.1, bf16[256,1024]{1,0:T(8,128)(2,1)} %refs_1_.1, bf16[256,256]{1,0:T(8,128)(2,1)} %refs_2_.2, bf16[256,256]{1,0:T(8,128)(2,1)} %refs_3_.2, bf16[256,1024]{1,0:T(8,128)(2,1)} %refs_4_.2, ...), custom_call_target="tpu_custom_call" | custom-call | flops 3758096384 | bytes 8388608 | tf_op jit(solution)/shard_map/pallas_call | solution.py:441
  56.8 2.1 %shard_map.225 = (f32[16,2048]{1,0:T(8,128)}, f32[16,2048]{1,0:T(8,128)}, f32[16,1024]{1,0:T(8,128)}, f32[16,1024]{1,0:T(8,128)}, f32[16,2048]{1,0:T(8,128)}, /*...) custom-call(bf16[8,2,16,128]{3,2,1,0:T(8,128)(2,1)} %get-tuple-element.10.refs_0_, ...), custom_call_target="tpu_custom_call" | custom-call | tf_op jit(solution)/shard_map/pallas_call | solution.py:483
